TPU v7x, 32 devices: a whole 2x2x4 slice. The times are simulated.
32 devices in a mesh: dp: 4 (over x, core), enc: 8 (over z, y).
Axes of the slice: x: 2, y: 2, z: 4, core: 2. Of those that a mesh axis runs over, the one named last changes fastest.
Arguments:
- counts: int32 [4, 8], P('dp'), may hold values from 1 to 48, 192 in all within a row
- pixels: bfloat16 [4, 6144, 392], P('dp', 'enc'), may hold values from -6 to 6
- cotangent: bfloat16 [4, 3072, 1728], P('dp', 'enc'), may hold values from -0.078125 to 0.078125
Outputs:
- grad_patch: float32 [1728, 392], P('enc')
Inputs may be any that keep to these rules, and one draw needn't show every extreme that they name: `counts`: each row of a group sums to exactly 192; in each row some device holds exactly 48 live blocks.
All inputs are finite; a program needn't handle non-finite values.
Results may differ from a plain program's by a relative error of at most 0.0003.
Values may be sent and summed in bfloat16 or wider, within the bound.
A program may use at most 64 MiB of HBM per device.

v0:
```python
import jax
import jax.numpy as jnp
from jax import lax
from jax.sharding import PartitionSpec as P

BLK = 16


def lookup(table, index, peers):
    return jnp.sum(jnp.where(index[:, None] == peers[None, :], table[None, :], 0), axis=1)


def per_device(counts, pixels, cotangent):
    n_enc = lax.axis_size("enc")
    me_enc = lax.axis_index("enc")
    group_counts = counts[0]
    starts = jnp.cumsum(group_counts) - group_counts
    peers = jnp.arange(n_enc, dtype=jnp.int32)
    own_count = jnp.sum(jnp.where(peers == me_enc, group_counts, 0))
    own_start = jnp.sum(jnp.where(peers == me_enc, starts, 0))
    slots = pixels.shape[1] // BLK
    width = pixels.shape[2]
    per_peer = max(1, slots // n_enc)
    slot_ids = jnp.arange(slots, dtype=jnp.int32)
    global_ids = own_start + slot_ids
    target = global_ids % n_enc * per_peer + slot_ids // n_enc
    columns = jnp.arange(n_enc * per_peer, dtype=jnp.int32)
    select = (columns[:, None] == target[None, :]) & (slot_ids < own_count)[None, :]
    blocks = pixels[0].reshape(slots, BLK * width)
    outgoing = jnp.dot(
        select.astype(jnp.bfloat16), blocks, preferred_element_type=jnp.float32
    ).astype(jnp.bfloat16)
    arrived = lax.all_to_all(outgoing, "enc", split_axis=0, concat_axis=0, tiled=True)
    source = columns // per_peer
    rank = columns % per_peer
    src_start = lookup(starts, source, peers)
    src_count = lookup(group_counts, source, peers)
    first_slot = (me_enc - src_start) % n_enc
    slot_there = first_slot + rank * n_enc
    valid = slot_there < src_count
    compact = (src_start + slot_there) // n_enc
    own_blocks = cotangent.shape[1] // BLK
    compact_ids = jnp.arange(own_blocks, dtype=jnp.int32)
    order = (compact_ids[:, None] == compact[None, :]) & valid[None, :]
    owned = jnp.dot(order.astype(jnp.bfloat16), arrived, preferred_element_type=jnp.float32).astype(
        jnp.bfloat16
    )
    owned = owned.reshape(own_blocks * BLK, width)
    cot_rows = cotangent[0]
    local = lax.psum_scatter(
        lax.dot_general(
            cot_rows, owned, (((0,), (0,)), ((), ())), preferred_element_type=jnp.float32
        ),
        "enc",
        scatter_dimension=0,
        tiled=True,
    )
    return lax.psum(local, "dp")


def solution(mesh):
    placed = (P("dp", None), P("dp", "enc", None), P("dp", "enc", None))
    return jax.shard_map(
        per_device, mesh=mesh, in_specs=placed, out_specs=P("enc", None), check_vma=False
    )
```

profile of v0, /device:TPU:0, one launch (start us, length us, event | category | flops | bytes accessed | tf_op | source)
XLA Modules:
  0.0 171.7 jit_solution(8669749628123273757)
XLA Ops:
  6.5 0.0 copy-start
  6.5 0.9 reduce-window.4
  7.5 1.4 fusion.13
  8.8 0.6 iota_compare_fusion.3
  9.5 0.7 fusion.11
  10.2 1.3 copy.6
  11.6 0.9 reshape_squeeze.3
  12.5 0.3 convolution_convert_fusion
  12.8 0.0 copy-start.1
  12.8 1.1 all_to_all.8
  13.9 7.3 %all-to-all-start = ((bf16[8,6,6272]{2,1,0:T(8,128)(2,1)}), bf16[8,6,6272]{2,1,0:T(8,128)(2,1)S(1)}, u32[]{:S(2)}, u32[]{:S(2)}) async-start(bf16[8,6,6272]{2,1,0:T(8,128)(2,1)} %all_to_all.8), calls=%async_computation | async-start | bytes 1605632 | tf_op jit(solution)/shard_map/all_to_all | solution.py:33
  21.2 0.0 reduce-scatter.4.cloned.1.call-start
  21.2 0.0 copy-done.1
  21.3 0.1 select_reduce_fusion
  21.4 20.3 %all-to-all-done = bf16[8,6,6272]{2,1,0:T(8,128)(2,1)S(1)} async-done(((bf16[8,6,6272]{2,1,0:T(8,128)(2,1)}), bf16[8,6,6272]{2,1,0:T(8,128)(2,1)S(1)}, u32[]{:S(2)}, u32[]{:S(2)}) %all-to-all-start) | async-done | bytes 602144 | tf_op jit(solution)/shard_map/all_to_all | solution.py:33
  41.7 0.2 all_to_all.10
  42.0 0.2 convolution_convert_fusion.1
  42.2 0.9 reshape.113
  43.1 0.0 copy-done
  43.1 2.5 %convolution_bitcast_fusion = f32[1728,392]{0,1:T(8,128)} fusion(bf16[384,392]{1,0:T(8,128)(2,1)S(1)} %reshape.113, bf16[1,384,1728]{1,2,0:T(8,128)(2,1)S(1)} %copy-done), kind=kOutput, calls=%fused_computation.2 | convolution fusion | flops 520224768 | bytes 4337664 | tf_op jit(solution)/shard_map/dot_general | solution.py:51
  45.6 4.7 %copy.7 = f32[1728,392]{1,0:T(8,128)} copy(f32[1728,392]{0,1:T(8,128)} %convolution_bitcast_fusion) | data formatting | bytes 5419008
  50.3 0.0 reduce-scatter.4.cloned.1.call-update
  50.3 0.0 all-reduce.2.cloned.1.call-start
  50.4 78.6 %reduce-scatter.4.cloned.1.call-done = f32[216,392]{1,0:T(8,128)} async-done(((f32[1728,392]{1,0:T(8,128)}), f32[216,392]{1,0:T(8,128)}) %reduce-scatter.4.cloned.1.call-update) | async-done | bytes 338704
  129.0 1.9 %copy.8 = f32[216,392]{0,1:T(8,128)} copy(f32[216,392]{1,0:T(8,128)} %reduce-scatter.4.cloned.1.call-done) | data formatting | bytes 677376
  130.9 0.0 all-reduce.2.cloned.1.call-update
  130.9 32.2 %all-reduce.2.cloned.1.call-done = f32[216,392]{0,1:T(8,128)} async-done(((f32[216,392]{0,1:T(8,128)}), f32[216,392]{0,1:T(8,128)}) %all-reduce.2.cloned.1.call-update) | async-done | bytes 338704 | tf_op jit(solution)/shard_map/psum | solution.py:58
  163.1 1.8 %copy.10 = f32[216,392]{0,1:T(8,128)} copy(f32[216,392]{0,1:T(8,128)} %all-reduce.2.cloned.1.call-done) | data formatting | bytes 677376
  (4 shorter events, 0.0 us)
Async XLA Ops:
  6.5 36.5 %copy-start = (bf16[1,384,1728]{1,2,0:T(8,128)(2,1)S(1)}, bf16[1,384,1728]{1,2,0:T(8,128)(2,1)}, u32[]{:S(2)}) copy-start(bf16[1,384,1728]{1,2,0:T(8,128)(2,1)} %param.5) | copy-start | bytes 3981316
  12.8 8.5 %copy-start.1 = (s32[1,8]{1,0:T(1,128)S(1)}, s32[1,8]{1,0:T(1,128)}, u32[]{:S(2)}) copy-start(s32[1,8]{1,0:T(1,128)} %param.3) | copy-start | bytes 100
  13.9 27.8 %all-to-all-start = ((bf16[8,6,6272]{2,1,0:T(8,128)(2,1)}), bf16[8,6,6272]{2,1,0:T(8,128)(2,1)S(1)}, u32[]{:S(2)}, u32[]{:S(2)}) async-start(bf16[8,6,6272]{2,1,0:T(8,128)(2,1)} %all_to_all.8), calls=%async_computation | async-start | bytes 1605632 | tf_op jit(solution)/shard_map/all_to_all | solution.py:33
  21.2 107.8 %reduce-scatter.4.cloned.1.call-start = ((), (), s32[]{:S(2)}) async-start(), calls=%async_computation.3 | async-start | bytes 3981312
  50.3 112.8 %all-reduce.2.cloned.1.call-start = ((), (), s32[]{:S(2)}) async-start(), calls=%async_computation.2 | async-start | bytes 802816 | tf_op jit(solution)/shard_map/psum | solution.py:58
Sparse Core Ops, SparseCore 0:
  50.5 78.4 reduce-scatter.3
  131.4 31.7 all-reduce.1
where the time goes:
time: 172 us
  waiting for transfers between devices  131 us (76%)
  between operations  13.5 us (8%)
  local copies, waits for them, and re-layouts  12.9 us (8%)
  starting transfers between devices  7.36 us (4%)
  other arithmetic  3.79 us (2%)
  matrix products  3.05 us (2%)
    unnamed x3, waiting for transfers between devices  78.6 us
    psum x1, waiting for transfers between devices, per_device(): return lax.psum(local, 'dp')  32.2 us
    all_to_all x1, waiting for transfers between devices, per_device(): lax.all_to_all(outgoing, 'enc', split_axis=0, concat_axis=0, tiled=True)  20.3 us
    unnamed x8, local copies, waits for them, and re-layouts  9.75 us
    all_to_all x1, starting transfers between devices, per_device(): lax.all_to_all(outgoing, 'enc', split_axis=0, concat_axis=0, tiled=True)  7.28 us
  transfers between devices with their start and end apart: 3, of which 3 were waited for; matrix products, arithmetic and copies ran while one was open for 0% of the time, Pallas kernels for 0%

commit v1 on v0

--- a/solution.py
+++ b/solution.py
@@ -1,9 +1,14 @@
+import functools
 import jax
 import jax.numpy as jnp
 from jax import lax
+from jax.experimental import pallas as pl
+from jax.experimental.pallas import tpu as pltpu
 from jax.sharding import PartitionSpec as P
 
 BLK = 16
+LANES = 128
+MESH = pl.DeviceIdType.MESH
 
 
 def lookup(table, index, peers):
@@ -14,8 +19,8 @@
     n_enc = lax.axis_size("enc")
     me_enc = lax.axis_index("enc")
     group_counts = counts[0]
-    starts = jnp.cumsum(group_counts) - group_counts
     peers = jnp.arange(n_enc, dtype=jnp.int32)
+    starts = jnp.sum(jnp.where(peers[None, :] < peers[:, None], group_counts[None, :], 0), axis=1)
     own_count = jnp.sum(jnp.where(peers == me_enc, group_counts, 0))
     own_start = jnp.sum(jnp.where(peers == me_enc, starts, 0))
     slots = pixels.shape[1] // BLK
@@ -58,8 +63,278 @@
     return lax.psum(local, "dp")
 
 
+def bits_of(number):
+    return number.bit_length() - 1
+
+
+def up(value, step):
+    return -(-value // step) * step
+
+
+def orders(ebits):
+    near = [ebits, 0] + ([1] if ebits > 1 else [])
+    far = list(range(2, ebits))
+    return [near[i:] + near[:i] + far for i in range(len(near))]
+
+
+def kernel(n_enc, plan, counts, pix, cot, out, *scratch):
+    ebits = bits_of(n_enc)
+    n_dp = 4
+    per_peer = pix.shape[0]
+    depth, own_rows = cot.shape
+    rows = depth // n_enc
+    half = up(up(rows, 2) // 2, 16)
+    quarter = half // 2
+    n_blocks = own_rows // BLK
+    pieces = len(plan)
+    it = iter(scratch)
+    outgoing, arrived, owned, cot_other, part, place = (next(it) for _ in range(6))
+    final, gathered = next(it), next(it)
+    a2a_send, a2a_recv, core_send, core_recv, rs_send, rs_recv, dp_send, dp_recv = (next(it) for _ in range(8))
+    work = [next(it) for _ in range(pieces)]
+    landed, reduced = [], []
+    for p in range(pieces):
+        landed.append([next(it) for _ in range(ebits + 1)])
+        reduced.append([next(it) for _ in range(ebits)])
+
+    me = lax.axis_index("enc")
+    dp = lax.axis_index("dp")
+    core, x = lax.rem(dp, 2), dp // 2
+
+    def enc_peer(j):
+        peer = me
+        for b in range(ebits):
+            if (j >> b) & 1:
+                peer = peer + (1 << b) - 2 * (1 << b) * lax.rem(me // (1 << b), 2)
+        return peer
+
+    def dp_peer(j):
+        peer = dp
+        for b in range(2):
+            if (j >> b) & 1:
+                peer = peer + (1 << b) - 2 * (1 << b) * lax.rem(dp // (1 << b), 2)
+        return peer
+
+    barrier = pltpu.get_barrier_semaphore()
+    for j in range(1, n_enc):
+        pl.semaphore_signal(barrier, inc=1, device_id=(dp, enc_peer(j)), device_id_type=MESH)
+    for j in range(1, n_dp):
+        pl.semaphore_signal(barrier, inc=1, device_id=(dp_peer(j), me), device_id_type=MESH)
+
+    start = jnp.int32(0)
+    for e in range(n_enc):
+        start = start + jnp.where(e < me, counts[0, e], 0)
+    start = lax.rem(start, n_enc)
+    for d in range(n_enc):
+        outgoing[d] = pix[:, lax.rem(d + n_enc - start, n_enc)]
+
+    pl.semaphore_wait(barrier, n_enc + n_dp - 2)
+    a2a = []
+    for j in reversed(range(1, n_enc)):
+        peer = enc_peer(j)
+        copy = pltpu.make_async_remote_copy(
+            src_ref=outgoing.at[peer],
+            dst_ref=arrived.at[pl.ds(me * per_peer, per_peer)],
+            send_sem=a2a_send.at[j - 1],
+            recv_sem=a2a_recv.at[j - 1],
+            device_id=(dp, peer),
+            device_id_type=MESH,
+        )
+        copy.start()
+        a2a.append(copy)
+
+    core_cot = pltpu.make_async_remote_copy(
+        src_ref=cot,
+        dst_ref=cot_other,
+        send_sem=core_send.at[0],
+        recv_sem=core_recv.at[0],
+        device_id=(dp_peer(1), me),
+        device_id_type=MESH,
+    )
+    core_cot.start()
+
+    def find(c, carry):
+        g = c * n_enc + me
+        source, first, end = jnp.int32(0), jnp.int32(0), jnp.int32(0)
+        for e in range(n_enc):
+            end = end + counts[0, e]
+            past = end <= g
+            source = source + jnp.where(past, 1, 0)
+            first = jnp.where(past, end, first)
+        place[c] = jnp.minimum(source * per_peer + (g - first) // n_enc, n_enc * per_peer - 1)
+        return carry
+
+    lax.fori_loop(0, n_blocks, find, 0)
+    arrived[pl.ds(me * per_peer, per_peer)] = outgoing[me]
+    for copy in a2a:
+        copy.wait_recv()
+    for c in range(n_blocks):
+        owned[c * BLK : (c + 1) * BLK, :] = arrived[place[c]]
+    core_pix = pltpu.make_async_remote_copy(
+        src_ref=owned.at[pl.ds(0, own_rows)],
+        dst_ref=owned.at[pl.ds(own_rows, own_rows)],
+        send_sem=core_send.at[1],
+        recv_sem=core_recv.at[1],
+        device_id=(dp_peer(1), me),
+        device_id_type=MESH,
+    )
+    core_pix.start()
+    core_cot.wait_recv()
+    core_pix.wait_recv()
+
+    base = core * (rows - half)
+    for i in range(n_enc // 2):
+        these = slice(2 * rows * i, 2 * rows * (i + 1))
+        part[...] = jnp.dot(
+            cot[these, :], owned[:own_rows, :], preferred_element_type=jnp.float32
+        ) + jnp.dot(cot_other[these, :], owned[own_rows:, :], preferred_element_type=jnp.float32)
+        for j in range(2):
+            e = 2 * i + j
+            index = tuple((e >> b) & 1 for b in reversed(range(ebits)))
+            for h in range(2):
+                at = pl.ds(pl.multiple_of(rows * j + base + quarter * h, 8), quarter)
+                for p, (low, wide, _) in enumerate(plan):
+                    work[p][index + (h,)] = part[at, low : low + wide]
+
+    def axis_of(a):
+        if a == ebits:
+            return x, (dp_peer(2), me)
+        return lax.rem(me // (1 << a), 2), (dp, enc_peer(1 << a))
+
+    held = list(work)
+    left = [list(reversed(range(ebits))) + [ebits] for _ in range(pieces)]
+    copies = [[] for _ in range(pieces)]
+
+    def send(p, s):
+        a = plan[p][2][s]
+        mine, other = axis_of(a)
+        ahead = (slice(None),) * left[p].index(a)
+        copy = pltpu.make_async_remote_copy(
+            src_ref=held[p].at[ahead + (1 - mine,)],
+            dst_ref=landed[p][s],
+            send_sem=rs_send.at[p, s],
+            recv_sem=rs_recv.at[p, s],
+            device_id=other,
+            device_id_type=MESH,
+        )
+        copy.start()
+        copies[p].append(copy)
+
+    for p in range(pieces):
+        send(p, 0)
+    for s in range(ebits + 1):
+        for p in range(pieces):
+            low, wide, order = plan[p]
+            a = order[s]
+            mine, _ = axis_of(a)
+            ahead = (slice(None),) * left[p].index(a)
+            copies[p][s].wait_recv()
+            total = held[p][ahead + (mine,)] + landed[p][s][...]
+            if s < ebits:
+                reduced[p][s][...] = total
+                held[p] = reduced[p][s]
+                left[p].remove(a)
+                send(p, s + 1)
+            else:
+                final[:, low : low + wide] = total
+
+    last = []
+    for j in range(1, n_dp):
+        copy = pltpu.make_async_remote_copy(
+            src_ref=final,
+            dst_ref=gathered.at[dp],
+            send_sem=dp_send.at[j - 1],
+            recv_sem=dp_recv.at[j - 1],
+            device_id=(dp_peer(j), me),
+            device_id_type=MESH,
+        )
+        copy.start()
+        last.append(copy)
+    gathered[dp] = final[...]
+    for copy in last:
+        copy.wait_recv()
+    for d in range(n_dp):
+        first = (d % 2) * (rows - half) + (d // 2) * quarter
+        out[first : first + quarter, :] = gathered[d]
+    for copy in a2a + [core_cot, core_pix] + sum(copies, []) + last:
+        copy.wait_send()
+
+
+def per_device_fused(n_enc, counts, pixels, cotangent):
+    ebits = bits_of(n_enc)
+    own_rows, depth = cotangent.shape[1:]
+    width = pixels.shape[2]
+    rows = depth // n_enc
+    half = up(up(rows, 2) // 2, 16)
+    quarter = half // 2
+    slots = pixels.shape[1] // BLK
+    per_peer = slots // n_enc
+    turns = orders(ebits)
+    plan = [
+        (low, min(LANES, width - low), turns[i % len(turns)]) for i, low in enumerate(range(0, width, LANES))
+    ]
+    f32, bf16 = jnp.float32, jnp.bfloat16
+    shapes = [
+        pltpu.VMEM((n_enc, per_peer, BLK, width), bf16),
+        pltpu.VMEM((slots, BLK, width), bf16),
+        pltpu.VMEM((2 * own_rows, width), bf16),
+        pltpu.VMEM((depth, own_rows), bf16),
+        pltpu.VMEM((2 * rows, width), f32),
+        pltpu.SMEM((own_rows // BLK,), jnp.int32),
+        pltpu.VMEM((quarter, width), f32),
+        pltpu.VMEM((4, quarter, width), f32),
+        pltpu.SemaphoreType.DMA((n_enc - 1,)),
+        pltpu.SemaphoreType.DMA((n_enc - 1,)),
+        pltpu.SemaphoreType.DMA((2,)),
+        pltpu.SemaphoreType.DMA((2,)),
+        pltpu.SemaphoreType.DMA((len(plan), ebits + 1)),
+        pltpu.SemaphoreType.DMA((len(plan), ebits + 1)),
+        pltpu.SemaphoreType.DMA((3,)),
+        pltpu.SemaphoreType.DMA((3,)),
+    ]
+    shapes += [pltpu.VMEM((2,) * (ebits + 1) + (quarter, wide), f32) for _, wide, _ in plan]
+    for _, wide, _ in plan:
+        shapes += [pltpu.VMEM((2,) * (ebits - s) + (quarter, wide), f32) for s in range(ebits + 1)]
+        shapes += [pltpu.VMEM((2,) * (ebits - s) + (quarter, wide), f32) for s in range(ebits)]
+    return pl.pallas_call(
+        functools.partial(kernel, n_enc, plan),
+        out_shape=jax.ShapeDtypeStruct((rows, width), f32),
+        in_specs=[
+            pl.BlockSpec(memory_space=pltpu.SMEM),
+            pl.BlockSpec(memory_space=pltpu.VMEM),
+            pl.BlockSpec(memory_space=pltpu.VMEM),
+        ],
+        out_specs=pl.BlockSpec(memory_space=pltpu.VMEM),
+        scratch_shapes=shapes,
+        compiler_params=pltpu.CompilerParams(
+            collective_id=0, has_side_effects=True, vmem_limit_bytes=48 * 1024 * 1024
+        ),
+    )(counts, pixels[0].reshape(per_peer, n_enc, BLK, width), cotangent[0].T)
+
+
+def fits(mesh, shapes):
+    n_enc, n_dp = mesh.shape["enc"], mesh.shape["dp"]
+    pixels, cotangent = shapes
+    slots, own_rows, depth = pixels[1] // n_enc // BLK, cotangent[1] // n_enc, cotangent[2]
+    return (
+        n_dp == 1 << 2
+        and n_enc > 1
+        and n_enc == 1 << bits_of(n_enc)
+        and slots % n_enc == 0
+        and own_rows % LANES == 0
+        and depth % (8 * n_enc) == 0
+        and depth * pixels[2] * 4 < 4 * 1024 * 1024
+    )
+
+
 def solution(mesh):
     placed = (P("dp", None), P("dp", "enc", None), P("dp", "enc", None))
-    return jax.shard_map(
-        per_device, mesh=mesh, in_specs=placed, out_specs=P("enc", None), check_vma=False
-    )
+
+    def run(counts, pixels, cotangent):
+        fused = fits(mesh, (pixels.shape, cotangent.shape))
+        body = functools.partial(per_device_fused, mesh.shape["enc"]) if fused else per_device
+        return jax.shard_map(
+            body, mesh=mesh, in_specs=placed, out_specs=P("enc", None), check_vma=False
+        )(counts, pixels, cotangent)
+
+    return run

time: 172 us -> 59.8 us (0.35)
  waiting for transfers between devices: 131 us -> 0 us
  Pallas kernels: 0 us -> 57.2 us
  between operations: 13.5 us -> 0.02 us
  local copies, waits for them, and re-layouts: 12.9 us -> 2.42 us
  starting transfers between devices: 7.36 us -> 0 us
  other arithmetic: 3.79 us -> 0 us
  matrix products: 3.05 us -> 0 us
    unnamed x3 -> x0, waiting for transfers between devices: 78.6 us -> none
    pallas_call x0 -> x1, Pallas kernels: none -> 57.2 us  [per_device_fused(): pl.pallas_call(functools.partial(kernel, n_enc, plan), out_shape=jax.Shap...]
    psum x1 -> x0, waiting for transfers between devices: 32.2 us -> none  [per_device(): return lax.psum(local, 'dp')]
    all_to_all x1 -> x0, waiting for transfers between devices: 20.3 us -> none  [per_device(): lax.all_to_all(outgoing, 'enc', split_axis=0, concat_axis=0, tiled=True)]
    unnamed x8 -> x5, local copies, waits for them, and re-layouts: 9.75 us -> 1.5 us
    all_to_all x1 -> x0, starting transfers between devices: 7.28 us -> none  [per_device(): lax.all_to_all(outgoing, 'enc', split_axis=0, concat_axis=0, tiled=True)]
    dot_general x3 -> x0, matrix products: 3.05 us -> none  [the longest x1 2.53 us: per_device(): lax.dot_general(cot_rows, owned, (((0,), (0,)), ((), ())), preferred_elem...]
  transfers between devices with their start and end apart: 3 -> 0, of which waited for: 3 -> 0; matrix products, arithmetic and copies ran while one was open for 0% -> 0% of each run, Pallas kernels for 0% -> 0%
where the time goes in v1:
time: 59.8 us; the launch traced here: 59.7 us
  Pallas kernels  57.2 us (96%)
  local copies, waits for them, and re-layouts  2.42 us (4%)
    pallas_call x1, Pallas kernels, per_device_fused(): pl.pallas_call(functools.partial(kernel, n_enc, plan), out_shape=jax.Shap...  57.2 us
    unnamed x5, local copies, waits for them, and re-layouts  1.5 us

profile of v1, /device:TPU:0, one launch (start us, length us, event | category | flops | bytes accessed | tf_op | source)
XLA Modules:
  0.0 59.7 jit_solution(6912057883074416076)
XLA Ops:
  0.0 0.0 copy-start
  0.0 0.0 copy-start.1
  0.0 1.4 %copy.4 = bf16[1,768,392]{2,1,0:T(8,128)(2,1)S(1)} copy(bf16[1,768,392]{1,2,0:T(8,128)(2,1)} %param.4) | data formatting | bytes 1204224 | tf_op args[1]
  1.5 0.0 copy-done
  1.5 0.0 copy-done.1
  1.5 57.2 %shard_map.37 = f32[216,392]{1,0:T(8,128)S(1)} custom-call(s32[1,8]{1,0:T(1,128)S(1)} %copy-done.1, bf16[6,8,16,392]{3,2,1,0:T(8,128)(2,1)S(1)} %bitcast.4, bf16[1728,384]{1,0:T(8,128)(2,1)S(1)} %bitcast.5), custom_call_target="tpu_custom_call" | custom-call | tf_op jit(solution)/shard_map/pallas_call | solution.py:299
  58.7 0.9 %copy.5 = f32[216,392]{0,1:T(8,128)} copy(f32[216,392]{1,0:T(8,128)S(1)} %shard_map.37) | data formatting | bytes 677376 | tf_op jit(solution)/shard_map/pallas_call | solution.py:299
Async XLA Ops:
  0.0 1.5 %copy-start = (bf16[1,384,1728]{1,2,0:T(8,128)(2,1)S(1)}, bf16[1,384,1728]{1,2,0:T(8,128)(2,1)}, u32[]{:S(2)}) copy-start(bf16[1,384,1728]{1,2,0:T(8,128)(2,1)} %param.5) | copy-start | bytes 3981316
  0.0 1.5 %copy-start.1 = (s32[1,8]{1,0:T(1,128)S(1)}, s32[1,8]{1,0:T(1,128)}, u32[]{:S(2)}) copy-start(s32[1,8]{1,0:T(1,128)} %counts.1) | copy-start | bytes 100

commit v2 on v0

--- a/solution.py
+++ b/solution.py
@@ -1,9 +1,14 @@
+import functools
 import jax
 import jax.numpy as jnp
 from jax import lax
+from jax.experimental import pallas as pl
+from jax.experimental.pallas import tpu as pltpu
 from jax.sharding import PartitionSpec as P
 
 BLK = 16
+LANES = 128
+MESH = pl.DeviceIdType.MESH
 
 
 def lookup(table, index, peers):
@@ -14,8 +19,8 @@
     n_enc = lax.axis_size("enc")
     me_enc = lax.axis_index("enc")
     group_counts = counts[0]
-    starts = jnp.cumsum(group_counts) - group_counts
     peers = jnp.arange(n_enc, dtype=jnp.int32)
+    starts = jnp.sum(jnp.where(peers[None, :] < peers[:, None], group_counts[None, :], 0), axis=1)
     own_count = jnp.sum(jnp.where(peers == me_enc, group_counts, 0))
     own_start = jnp.sum(jnp.where(peers == me_enc, starts, 0))
     slots = pixels.shape[1] // BLK
@@ -58,8 +63,299 @@
     return lax.psum(local, "dp")
 
 
+def bits_of(number):
+    return number.bit_length() - 1
+
+
+def up(value, step):
+    return -(-value // step) * step
+
+
+def orders(ebits, pieces):
+    return [[ebits] + list(range(ebits)) for _ in range(pieces)]
+
+
+def sizes(n_enc, slots, own_rows, depth, width):
+    rows = depth // n_enc
+    half = up(up(rows, 2) // 2, 16)
+    pieces = width // LANES
+    return rows, half, half // 2, slots // n_enc, pieces, width % LANES
+
+
+def kernel(n_enc, counts, pix, cot, out, *scratch):
+    ebits = bits_of(n_enc)
+    n_dp = 4
+    depth, own_rows = cot.shape
+    rows, half, quarter, per_peer, pieces, tail = sizes(n_enc, pix.shape[0] * n_enc, own_rows, depth, pix.shape[3])
+    low_tail = pieces * LANES
+    stages = ebits + 1
+    plan = orders(ebits, pieces)
+    n_blocks = own_rows // BLK
+    it = iter(scratch)
+    cot_other, source_of, slot_of, tails = (next(it) for _ in range(4))
+    a2a_send, a2a_recv, cot_send, cot_recv, pix_send, pix_recv, rs_send, rs_recv, dp_send, dp_recv = (
+        next(it) for _ in range(10)
+    )
+    outgoing, arrived, owned, part, work, final, gathered = ([next(it) for _ in range(pieces)] for _ in range(7))
+    landed = [[next(it) for _ in range(stages)] for _ in range(pieces)]
+    reduced = [[next(it) for _ in range(ebits)] for _ in range(pieces)]
+    chunk = [ref.shape[0] // n_enc for ref in arrived]
+
+    me = lax.axis_index("enc")
+    dp = lax.axis_index("dp")
+    core, x = lax.rem(dp, 2), dp // 2
+
+    def flipped(index, j, bits):
+        for b in range(bits):
+            if (j >> b) & 1:
+                index = index + (1 << b) - 2 * (1 << b) * lax.rem(index // (1 << b), 2)
+        return index
+
+    def enc_peer(j):
+        return flipped(me, j, ebits)
+
+    def dp_peer(j):
+        return flipped(dp, j, 2)
+
+    def remote(src, dst, send_sem, recv_sem, device):
+        copy = pltpu.make_async_remote_copy(
+            src_ref=src, dst_ref=dst, send_sem=send_sem, recv_sem=recv_sem, device_id=device, device_id_type=MESH
+        )
+        copy.start()
+        started.append(copy)
+        return copy
+
+    started = []
+    barrier = pltpu.get_barrier_semaphore()
+    for j in range(1, n_enc):
+        pl.semaphore_signal(barrier, inc=1, device_id=(dp, enc_peer(j)), device_id_type=MESH)
+    for j in range(1, n_dp):
+        pl.semaphore_signal(barrier, inc=1, device_id=(dp_peer(j), me), device_id_type=MESH)
+
+    start = jnp.int32(0)
+    for e in range(n_enc):
+        start = start + jnp.where(e < me, counts[0, e], 0)
+    start = lax.rem(start, n_enc)
+
+    def fill(p):
+        for d in range(n_enc):
+            r = lax.rem(d + n_enc - start, n_enc)
+            outgoing[p][d * chunk[p] : d * chunk[p] + per_peer] = pix[:, r, :, p * LANES : (p + 1) * LANES]
+            if p == 0:
+                for k in range(per_peer):
+                    outgoing[p][d * chunk[p] + per_peer, :, k * tail : (k + 1) * tail] = pix[k, r, :, low_tail:]
+
+    a2a = [[] for _ in range(pieces)]
+
+    def deal(p):
+        for j in reversed(range(1, n_enc)):
+            peer = enc_peer(j)
+            a2a[p].append(
+                remote(
+                    outgoing[p].at[pl.ds(peer * chunk[p], chunk[p])],
+                    arrived[p].at[pl.ds(me * chunk[p], chunk[p])],
+                    a2a_send.at[p, j - 1],
+                    a2a_recv.at[p, j - 1],
+                    (dp, peer),
+                )
+            )
+
+    fill(0)
+    pl.semaphore_wait(barrier, n_enc + n_dp - 2)
+    deal(0)
+    core_cot = remote(cot, cot_other, cot_send.at[0], cot_recv.at[0], (dp_peer(1), me))
+    for p in range(1, pieces):
+        fill(p)
+        deal(p)
+
+    def find(c, carry):
+        g = c * n_enc + me
+        source, first, end = jnp.int32(0), jnp.int32(0), jnp.int32(0)
+        for e in range(n_enc):
+            end = end + counts[0, e]
+            past = end <= g
+            source = source + jnp.where(past, 1, 0)
+            first = jnp.where(past, end, first)
+        source_of[c] = jnp.minimum(source, n_enc - 1)
+        slot_of[c] = jnp.minimum((g - first) // n_enc, per_peer - 1)
+        return carry
+
+    lax.fori_loop(0, n_blocks, find, 0)
+    base = core * (rows - half)
+
+    def axis_of(a):
+        if a == ebits:
+            return x, (dp_peer(2), me)
+        return lax.rem(me // (1 << a), 2), (dp, enc_peer(1 << a))
+
+    held = list(work)
+    left = [list(reversed(range(ebits))) + [ebits] for _ in range(pieces)]
+    copies = [[] for _ in range(pieces)]
+    last = [[] for _ in range(pieces)]
+
+    def send(p, s):
+        a = plan[p][s]
+        mine, other = axis_of(a)
+        ahead = (slice(None),) * left[p].index(a)
+        copies[p].append(
+            remote(held[p].at[ahead + (1 - mine,)], landed[p][s], rs_send.at[p, s], rs_recv.at[p, s], other)
+        )
+
+    def launch(p):
+        here = pl.ds(me * chunk[p], chunk[p])
+        arrived[p][here] = outgoing[p][here]
+        for copy in a2a[p]:
+            copy.wait_recv()
+        if p == 0:
+            for e in range(n_enc):
+                for k in range(per_peer):
+                    tails[e * per_peer + k] = arrived[p][e * chunk[p] + per_peer, :, k * tail : (k + 1) * tail]
+        for c in range(n_blocks):
+            these = slice(c * BLK, (c + 1) * BLK)
+            owned[p][these, :LANES] = arrived[p][source_of[c] * chunk[p] + slot_of[c]]
+            if p == 0:
+                owned[p][these, LANES:] = tails[source_of[c] * per_peer + slot_of[c]]
+        swap = remote(
+            owned[p].at[pl.ds(0, own_rows)],
+            owned[p].at[pl.ds(own_rows, own_rows)],
+            pix_send.at[p],
+            pix_recv.at[p],
+            (dp_peer(1), me),
+        )
+        if p == 0:
+            core_cot.wait_recv()
+        swap.wait_recv()
+        for i in range(n_enc // 2):
+            these = slice(2 * rows * i, 2 * rows * (i + 1))
+            part[p][...] = jnp.dot(
+                cot[these, :], owned[p][:own_rows, :], preferred_element_type=jnp.float32
+            ) + jnp.dot(cot_other[these, :], owned[p][own_rows:, :], preferred_element_type=jnp.float32)
+            for j in range(2):
+                e = 2 * i + j
+                index = tuple((e >> b) & 1 for b in reversed(range(ebits)))
+                for h in range(2):
+                    at = rows * j + base + quarter * h
+                    work[p][index + (h, slice(0, quarter))] = part[p][pl.ds(pl.multiple_of(at, 8), quarter), :LANES]
+                    if p == 0:
+                        for r in range(quarter // 8):
+                            work[p][index + (h, slice(quarter, quarter + 8), slice(r * tail, (r + 1) * tail))] = part[p][
+                                pl.ds(pl.multiple_of(at + 8 * r, 8), 8), LANES:
+                            ]
+        send(p, 0)
+
+    def advance(p, s):
+        a = plan[p][s]
+        mine, _ = axis_of(a)
+        ahead = (slice(None),) * left[p].index(a)
+        copies[p][s].wait_recv()
+        total = held[p][ahead + (mine,)] + landed[p][s][...]
+        if s < ebits:
+            reduced[p][s][...] = total
+            held[p] = reduced[p][s]
+            left[p].remove(a)
+            send(p, s + 1)
+            return
+        final[p][...] = total
+        for j in range(1, n_dp):
+            last[p].append(
+                remote(final[p], gathered[p].at[dp], dp_send.at[p, j - 1], dp_recv.at[p, j - 1], (dp_peer(j), me))
+            )
+        gathered[p][dp] = total
+
+    for tick in range(pieces + stages):
+        if tick < pieces:
+            launch(tick)
+        for p in range(pieces):
+            s = tick - p - 1
+            if 0 <= s < stages:
+                advance(p, s)
+    for p in range(pieces):
+        for copy in last[p]:
+            copy.wait_recv()
+        for d in range(n_dp):
+            first = (d % 2) * (rows - half) + (d // 2) * quarter
+            out[first : first + quarter, p * LANES : (p + 1) * LANES] = gathered[p][d, :quarter]
+            if p == 0:
+                for r in range(quarter // 8):
+                    out[first + 8 * r : first + 8 * r + 8, low_tail:] = gathered[p][
+                        d, quarter : quarter + 8, r * tail : (r + 1) * tail
+                    ]
+    for copy in started:
+        copy.wait_send()
+
+
+def per_device_fused(n_enc, counts, pixels, cotangent):
+    ebits = bits_of(n_enc)
+    own_rows, depth = cotangent.shape[1:]
+    width = pixels.shape[2]
+    slots = pixels.shape[1] // BLK
+    rows, half, quarter, per_peer, pieces, tail = sizes(n_enc, slots, own_rows, depth, width)
+    f32, bf16, dma = jnp.float32, jnp.bfloat16, pltpu.SemaphoreType.DMA
+    stages = ebits + 1
+    each = range(pieces)
+    chunk = [per_peer + (p == 0) for p in each]
+    wide = [LANES + tail * (p == 0) for p in each]
+    tall = [quarter + 8 * (p == 0) for p in each]
+    shapes = [
+        pltpu.VMEM((depth, own_rows), bf16),
+        pltpu.SMEM((own_rows // BLK,), jnp.int32),
+        pltpu.SMEM((own_rows // BLK,), jnp.int32),
+        pltpu.VMEM((slots, BLK, tail), bf16),
+    ]
+    for shape in ((pieces, n_enc - 1), (1,), (pieces,), (pieces, stages), (pieces, 3)):
+        shapes += [dma(shape), dma(shape)]
+    for _ in range(2):
+        shapes += [pltpu.VMEM((n_enc * chunk[p], BLK, LANES), bf16) for p in each]
+    shapes += [pltpu.VMEM((2 * own_rows, wide[p]), bf16) for p in each]
+    shapes += [pltpu.VMEM((2 * rows, wide[p]), f32) for p in each]
+    shapes += [pltpu.VMEM((2,) * stages + (tall[p], LANES), f32) for p in each]
+    shapes += [pltpu.VMEM((tall[p], LANES), f32) for p in each]
+    shapes += [pltpu.VMEM((4, tall[p], LANES), f32) for p in each]
+    for p in each:
+        shapes += [pltpu.VMEM((2,) * (ebits - s) + (tall[p], LANES), f32) for s in range(stages)]
+    for p in each:
+        shapes += [pltpu.VMEM((2,) * (ebits - s) + (tall[p], LANES), f32) for s in range(ebits)]
+    return pl.pallas_call(
+        functools.partial(kernel, n_enc),
+        out_shape=jax.ShapeDtypeStruct((rows, width), f32),
+        in_specs=[
+            pl.BlockSpec(memory_space=pltpu.SMEM),
+            pl.BlockSpec(memory_space=pltpu.VMEM),
+            pl.BlockSpec(memory_space=pltpu.VMEM),
+        ],
+        out_specs=pl.BlockSpec(memory_space=pltpu.VMEM),
+        scratch_shapes=shapes,
+        compiler_params=pltpu.CompilerParams(
+            collective_id=0, has_side_effects=True, vmem_limit_bytes=48 * 1024 * 1024
+        ),
+    )(counts, pixels[0].reshape(per_peer, n_enc, BLK, width), cotangent[0].T)
+
+
+def fits(mesh, shapes):
+    n_enc, n_dp = mesh.shape["enc"], mesh.shape["dp"]
+    pixels, cotangent = shapes
+    slots, own_rows, depth = pixels[1] // n_enc // BLK, cotangent[1] // n_enc, cotangent[2]
+    return (
+        n_dp == 1 << 2
+        and n_enc > 1
+        and n_enc == 1 << bits_of(n_enc)
+        and slots % n_enc == 0
+        and own_rows % LANES == 0
+        and depth % (8 * n_enc) == 0
+        and pixels[2] >= LANES
+        and 0 < pixels[2] % LANES * max(slots // n_enc, depth // n_enc // 16) <= LANES
+        and depth * pixels[2] * 4 < 4 * 1024 * 1024
+    )
+
+
 def solution(mesh):
     placed = (P("dp", None), P("dp", "enc", None), P("dp", "enc", None))
-    return jax.shard_map(
-        per_device, mesh=mesh, in_specs=placed, out_specs=P("enc", None), check_vma=False
-    )
+
+    def run(counts, pixels, cotangent):
+        fused = fits(mesh, (pixels.shape, cotangent.shape))
+        body = functools.partial(per_device_fused, mesh.shape["enc"]) if fused else per_device
+        return jax.shard_map(
+            body, mesh=mesh, in_specs=placed, out_specs=P("enc", None), check_vma=False
+        )(counts, pixels, cotangent)
+
+    return run

time: 172 us -> 53.8 us (0.31)
  waiting for transfers between devices: 131 us -> 0 us
  Pallas kernels: 0 us -> 51.2 us
  between operations: 13.5 us -> 0.02 us
  local copies, waits for them, and re-layouts: 12.9 us -> 2.42 us
  starting transfers between devices: 7.36 us -> 0 us
  other arithmetic: 3.79 us -> 0 us
  matrix products: 3.05 us -> 0 us
    unnamed x3 -> x0, waiting for transfers between devices: 78.6 us -> none
    pallas_call x0 -> x1, Pallas kernels: none -> 51.2 us  [per_device_fused(): pl.pallas_call(functools.partial(kernel, n_enc), out_shape=jax.ShapeDtype...]
    psum x1 -> x0, waiting for transfers between devices: 32.2 us -> none  [per_device(): return lax.psum(local, 'dp')]
    all_to_all x1 -> x0, waiting for transfers between devices: 20.3 us -> none  [per_device(): lax.all_to_all(outgoing, 'enc', split_axis=0, concat_axis=0, tiled=True)]
    unnamed x8 -> x5, local copies, waits for them, and re-layouts: 9.75 us -> 1.5 us
    all_to_all x1 -> x0, starting transfers between devices: 7.28 us -> none  [per_device(): lax.all_to_all(outgoing, 'enc', split_axis=0, concat_axis=0, tiled=True)]
    dot_general x3 -> x0, matrix products: 3.05 us -> none  [the longest x1 2.53 us: per_device(): lax.dot_general(cot_rows, owned, (((0,), (0,)), ((), ())), preferred_elem...]
  transfers between devices with their start and end apart: 3 -> 0, of which waited for: 3 -> 0; matrix products, arithmetic and copies ran while one was open for 0% -> 0% of each run, Pallas kernels for 0% -> 0%
where the time goes in v2:
time: 53.8 us; the launch traced here: 53.6 us
  Pallas kernels  51.2 us (95%)
  local copies, waits for them, and re-layouts  2.42 us (4%)
    pallas_call x1, Pallas kernels, per_device_fused(): pl.pallas_call(functools.partial(kernel, n_enc), out_shape=jax.ShapeDtype...  51.2 us
    unnamed x5, local copies, waits for them, and re-layouts  1.5 us

profile of v2, /device:TPU:0, one launch (start us, length us, event | category | flops | bytes accessed | tf_op | source)
XLA Modules:
  0.0 53.6 jit_solution(14712916716191044208)
XLA Ops:
  0.0 0.0 copy-start
  0.0 0.0 copy-start.1
  0.0 1.4 %copy.4 = bf16[1,768,392]{2,1,0:T(8,128)(2,1)S(1)} copy(bf16[1,768,392]{1,2,0:T(8,128)(2,1)} %param.4) | data formatting | bytes 1204224 | tf_op args[1]
  1.5 0.0 copy-done
  1.5 0.0 copy-done.1
  1.5 51.2 %shard_map.37 = f32[216,392]{1,0:T(8,128)S(1)} custom-call(s32[1,8]{1,0:T(1,128)S(1)} %copy-done.1, bf16[6,8,16,392]{3,2,1,0:T(8,128)(2,1)S(1)} %bitcast.4, bf16[1728,384]{1,0:T(8,128)(2,1)S(1)} %bitcast.5), custom_call_target="tpu_custom_call" | custom-call | tf_op jit(solution)/shard_map/pallas_call | solution.py:318
  52.7 0.9 %copy.5 = f32[216,392]{0,1:T(8,128)} copy(f32[216,392]{1,0:T(8,128)S(1)} %shard_map.37) | data formatting | bytes 677376 | tf_op jit(solution)/shard_map/pallas_call | solution.py:318
Async XLA Ops:
  0.0 1.5 %copy-start = (bf16[1,384,1728]{1,2,0:T(8,128)(2,1)S(1)}, bf16[1,384,1728]{1,2,0:T(8,128)(2,1)}, u32[]{:S(2)}) copy-start(bf16[1,384,1728]{1,2,0:T(8,128)(2,1)} %param.5) | copy-start | bytes 3981316
  0.0 1.5 %copy-start.1 = (s32[1,8]{1,0:T(1,128)S(1)}, s32[1,8]{1,0:T(1,128)}, u32[]{:S(2)}) copy-start(s32[1,8]{1,0:T(1,128)} %counts.1) | copy-start | bytes 100
